TPU v7x, 32 devices: a whole 2x2x4 slice. The times are simulated.
32 devices in a mesh: seq: 8 (over z, y), head: 4 (over x, core).
Axes of the slice: x: 2, y: 2, z: 4, core: 2. Of those that a mesh axis runs over, the one named last changes fastest.
Arguments:
- queries: bfloat16 [4096, 2048], P('seq', 'head'), may hold values from -4 to 4
- keys: bfloat16 [4096, 2048], P('seq', 'head'), may hold values from -4 to 4
- values: bfloat16 [4096, 2048], P('seq', 'head'), may hold values from -6 to 6
- rates: float32 [4096, 4], P('seq', 'head'), may hold values from 0.02 to 0.3
- fast: bfloat16 [4, 3, 512, 512], P('head'), may hold values from -0.25 to 0.25
- momentum: float32 [4, 3, 512, 512], P('head', None, 'seq'), may hold values from -0.24 to 0.24
- out_proj: bfloat16 [2048, 2048], P('seq', 'head'), may hold values from -0.125 to 0.125
Outputs:
- mixed: bfloat16 [4096, 2048], P('seq', 'head')
- new_momentum: float32 [4, 3, 512, 512], P('head', None, 'seq')
All inputs are finite; a program needn't handle non-finite values.
Results may differ from a plain program's by a relative error of at most 0.0094.
Values may be sent and summed in bfloat16 or wider, within the bound.
No kernel may reach another device: no remote copies, remote signals or barrier semaphores. Data moves between devices by JAX's collectives and lax.ppermute only.
A program may use at most 64 MiB of HBM per device.

v0:
```python
import functools
import math

import jax
import jax.numpy as jnp
import numpy as np
from jax import lax
from jax.experimental import pallas as pl
from jax.experimental.pallas import tpu as pltpu
from jax.sharding import PartitionSpec as P

HD = 512
WINDOW = 512

MOMENTUM_DECAY = 0.9
NORM_EPS = 1e-06
NEG_LARGE = -1e30
MIB = 1024 * 1024


def times_transposed(left, right):
    return lax.dot_general(
        left, right, (((1,), (1,)), ((), ())), preferred_element_type=jnp.float32
    )


def contract_rows(left, right):
    return lax.dot_general(
        left, right, (((0,), (0,)), ((), ())), preferred_element_type=jnp.float32
    )


def matmul(left, right):
    return jnp.dot(left, right, preferred_element_type=jnp.float32)


def swap(array, axis, mask):
    devices = lax.axis_size(axis)
    return lax.ppermute(array, axis, [(i, i ^ mask) for i in range(devices)])


def params(mib):
    return pltpu.CompilerParams(vmem_limit_bytes=mib * MIB)


def whole_spec():
    return pl.BlockSpec(memory_space=pltpu.VMEM)


def gradient_rows(outer, scale, side, k, v, r, w, eye, hg_s, hu_s, err_s, dg_s, du_s):
    tokens, hidden = k.shape
    own = hidden // (2 * outer)
    hg = times_transposed(w[0], k)
    hu = times_transposed(w[1], k)
    hg_s[...] = hg
    hu_s[...] = hu
    gated = (hg * jax.nn.sigmoid(hg) * hu).astype(jnp.bfloat16)
    turned = times_transposed(eye, v)
    err_s[...] = (-scale * r * turned).astype(jnp.bfloat16)
    down_t = times_transposed(eye, w[2]).astype(jnp.bfloat16)
    back = matmul(down_t, err_s[...])
    dg_s[2] = back
    errors = []
    for z in range(outer):
        rows = pl.ds(pl.multiple_of((2 * z + side) * own, own), own)
        to = pl.ds(z * own, own)
        g, u, b = hg_s[rows], hu_s[rows], dg_s[2, rows]
        s = jax.nn.sigmoid(g)
        du_s[0, to] = (b * u * s * (1.0 + g * (1.0 - s))).astype(jnp.bfloat16)
        du_s[1, to] = (b * g * s).astype(jnp.bfloat16)
        du_s[2, to] = err_s[rows]
    return (
        matmul(du_s[0], k),
        matmul(du_s[1], k),
        times_transposed(du_s[2], gated),
    )


def identity(size):
    rows = lax.broadcasted_iota(jnp.int32, (size, size), 0)
    columns = lax.broadcasted_iota(jnp.int32, (size, size), 1)
    return jnp.where(rows == columns, 1.0, 0.0).astype(jnp.bfloat16)


def own_kernel(outer, scale, place, k, v, r, w, acc, *scratch):
    eye = identity(v.shape[1])
    parts = gradient_rows(outer, scale, place[0], k[...], v[...], r[...], w[0], eye, *scratch)
    own = acc.shape[2]
    for i, part in enumerate(parts):
        acc[:, i] = part.reshape(outer, own, part.shape[1])


def both_kernel(outer, scale, place, k, v, r, w, acc, mine, *rest):
    sent, scratch = rest[: outer - 1], rest[outer - 1 :]
    eye = identity(v.shape[1])
    parts = gradient_rows(outer, scale, place[0], k[...], v[...], r[...], w[0], eye, *scratch)
    own = acc.shape[2]
    total = scratch[1]
    for i, part in enumerate(parts):
        total[pl.ds(0, outer * own), :] = part + acc[:, i].reshape(outer * own, part.shape[1])
        mine[i] = total[pl.ds(pl.multiple_of(place[1] * own, own), own), :]
        for step in range(1, outer):
            other = place[1] ^ step
            block = total[pl.ds(pl.multiple_of(other * own, own), own), :]
            sent[step - 1][i] = block.astype(jnp.bfloat16)


def gradient_scratch(tokens, hidden):
    return [
        pltpu.VMEM((hidden, tokens), jnp.float32),
        pltpu.VMEM((hidden, tokens), jnp.float32),
        pltpu.VMEM((hidden, tokens), jnp.bfloat16),
        pltpu.VMEM((3, hidden, tokens), jnp.float32),
        pltpu.VMEM((3, hidden // 2, tokens), jnp.bfloat16),
    ]


def gradient_cost(tokens, hidden):
    return pl.CostEstimate(
        flops=12 * tokens * hidden * hidden, bytes_accessed=4_000_000, transcendentals=0
    )


def own_gradients(place, k, v, r, w, outer, scale):
    tokens, hidden = k.shape
    own = hidden // (2 * outer)
    return pl.pallas_call(
        functools.partial(own_kernel, outer, scale),
        out_shape=jax.ShapeDtypeStruct((outer, 3, own, hidden), jnp.float32),
        in_specs=[pl.BlockSpec(memory_space=pltpu.SMEM)] + [whole_spec()] * 4,
        out_specs=whole_spec(),
        scratch_shapes=gradient_scratch(tokens, hidden),
        compiler_params=params(20),
        cost_estimate=gradient_cost(tokens, hidden),
        name="own_gradients",
    )(place, k, v, r, w)


def both_gradients(place, k, v, r, w, acc, outer, scale):
    tokens, hidden = k.shape
    own = hidden // (2 * outer)
    return pl.pallas_call(
        functools.partial(both_kernel, outer, scale),
        out_shape=[jax.ShapeDtypeStruct((3, own, hidden), jnp.float32)]
        + [jax.ShapeDtypeStruct((3, own, hidden), jnp.bfloat16)] * (outer - 1),
        in_specs=[pl.BlockSpec(memory_space=pltpu.SMEM)] + [whole_spec()] * 5,
        out_specs=[whole_spec()] * outer,
        scratch_shapes=gradient_scratch(tokens, hidden),
        compiler_params=params(20),
        cost_estimate=gradient_cost(tokens, hidden),
        name="both_gradients",
    )(place, k, v, r, w, acc)


def apply_kernel(count, origin, q, attended, *rest):
    units, combined, full = rest[:count], rest[count], rest[count + 1]
    own = units[0].shape[1]
    for i in range(count):
        rows = pl.ds(pl.multiple_of(origin[i] * own, own), own)
        full[:, rows, :] = units[i][...]
    b1 = times_transposed(q[...], full[0])
    b3 = times_transposed(q[...], full[1])
    fast_in = (b1 * jax.nn.sigmoid(b1) * b3).astype(jnp.bfloat16)
    out = times_transposed(fast_in, full[2])
    combined[...] = (attended[...] + out).astype(jnp.bfloat16)


def apply_fast(origin, q, attended, units):
    tokens, hidden = q.shape
    return pl.pallas_call(
        functools.partial(apply_kernel, len(units)),
        out_shape=jax.ShapeDtypeStruct((tokens, hidden), jnp.bfloat16),
        in_specs=[pl.BlockSpec(memory_space=pltpu.SMEM)] + [whole_spec()] * (2 + len(units)),
        out_specs=whole_spec(),
        scratch_shapes=[pltpu.VMEM((3, hidden, hidden), jnp.bfloat16)],
        compiler_params=params(14),
        cost_estimate=pl.CostEstimate(
            flops=6 * tokens * hidden * hidden, bytes_accessed=4_000_000, transcendentals=0
        ),
        name="apply_fast",
    )(origin, q, attended, *units)


def project_kernel(count, tags, blocks_in, last, origin, *rest):
    blocks, units = rest[:blocks_in], rest[blocks_in : blocks_in + 4]
    before = None if not last else rest[blocks_in + 4]
    total, full = rest[-2:]
    steps = count // 2
    rows_in = units[0].shape[0] * 2 // steps
    for i in range(count):
        part, at = divmod(i % steps, steps // 2)
        rows = pl.ds(pl.multiple_of(origin[i] * rows_in, rows_in), rows_in)
        full[rows, :] = units[2 * (i // steps) + part][pl.ds(at * rows_in, rows_in), :]
    width = blocks[0].shape[1]
    value = before[...] if last else None
    for block, tag in zip(blocks, tags):
        rows = pl.ds(pl.multiple_of((origin[count] ^ tag) * width, width), width)
        part = matmul(block[...], full[rows, :])
        value = part if value is None else value + part
    total[...] = value.astype(total.dtype)


def project(origin, blocks, tags, units, before=None):
    tokens = blocks[0].shape[0]
    count = origin.shape[0] - 1
    rows_in, width = sum(unit.shape[0] for unit in units), units[0].shape[1]
    last = before is not None
    return pl.pallas_call(
        functools.partial(project_kernel, count, tags, len(blocks), last),
        out_shape=jax.ShapeDtypeStruct((tokens, width), jnp.bfloat16 if last else jnp.float32),
        in_specs=[pl.BlockSpec(memory_space=pltpu.SMEM)]
        + [whole_spec()] * (4 + len(blocks) + last),
        out_specs=whole_spec(),
        scratch_shapes=[pltpu.VMEM((rows_in, width), jnp.bfloat16)],
        compiler_params=params(14),
        cost_estimate=pl.CostEstimate(
            flops=2 * tokens * HD * len(blocks) * width,
            bytes_accessed=4_000_000,
            transcendentals=0,
        ),
        name="project",
    )(origin, *blocks, *units, *([before] if last else []))


def ring_order(outer):
    return [0] + list(range(1, outer, 2)) + list(range(outer - 2 + outer % 2, 0, -2))


def ring_step(unit, outer):
    order = ring_order(outer)
    pairs = []
    for place, z in enumerate(order):
        to = order[(place + 1) % outer]
        pairs += [(2 * z + y, 2 * to + y) for y in range(2)]
    return lax.ppermute(unit, "seq", pairs)


def after(array, *others):
    return lax.optimization_barrier((array,) + others)[0]


def ring_origins(outer):
    order = ring_order(outer)
    table = []
    for s in range(2 * outer):
        place = order.index(s // 2)
        sources = [order[(place - step) % outer] for step in range(outer)]
        table.append([2 * z + s % 2 for z in sources] + [2 * z + 1 - s % 2 for z in sources])
    return np.array(table, np.int32)


def renormalize(base, moment):
    updated = base - moment
    base_rms = jnp.sqrt(jnp.mean(base * base, axis=-1, keepdims=True) + NORM_EPS)
    new_rms = jnp.sqrt(jnp.mean(updated * updated, axis=-1, keepdims=True) + NORM_EPS)
    return (updated * (base_rms / new_rms)).astype(jnp.bfloat16)


def attention(queries, keys, values, early_keys, early_values, position):
    tok_rows = queries.shape[0]
    all_keys = jnp.concatenate([early_keys, keys], axis=0)
    all_values = jnp.concatenate([early_values, values], axis=0)
    key_pos = (position - 1) * tok_rows + jnp.arange(all_keys.shape[0])
    query_pos = position * tok_rows + jnp.arange(tok_rows)
    spacing = query_pos[:, None] - key_pos[None, :]
    allowed = (spacing >= 0) & (spacing < WINDOW) & (key_pos[None, :] >= 0)
    scores = times_transposed(queries, all_keys) * (1.0 / math.sqrt(HD))
    scores = jnp.where(allowed, scores, NEG_LARGE)
    highest = jnp.max(scores, axis=1, keepdims=True)
    expo = jnp.exp(scores - highest)
    probs = (expo / jnp.sum(expo, axis=1, keepdims=True)).astype(jnp.bfloat16)
    return jnp.dot(probs, all_values, preferred_element_type=jnp.float32)


def shards(queries, keys, values, rates, fast, momentum, out_proj):
    tok_rows = queries.shape[0]
    ranks = lax.axis_size("seq")
    heads = lax.axis_size("head")
    position = lax.axis_index("seq")
    head = lax.axis_index("head")
    own_rows = momentum.shape[2]
    if own_rows % 16 or ranks % 4 or heads % 2:
        return plain(queries, keys, values, rates, fast, momentum, out_proj)
    outer = ranks // 2
    grad_scale = 1.0 / math.sqrt(tok_rows * ranks)
    place = jnp.stack([position % 2, position // 2]).astype(jnp.int32)
    origins = jnp.asarray(ring_origins(outer))[position]

    behind = [(i, (i + 1) % ranks) for i in range(ranks)]
    rates_row = rates.reshape(1, tok_rows)
    early_keys = lax.ppermute(keys, "seq", behind)
    early_values = lax.ppermute(values, "seq", behind)
    early_rates = lax.ppermute(rates_row, "seq", behind)

    acc = own_gradients(place, keys, values, rates_row, fast, outer, grad_scale)
    wide = [after(out_proj, acc)]
    for _ in range(1, outer):
        wide.append(ring_step(wide[-1], outer))
    half = outer // 2
    near_half = [jnp.concatenate(wide[:half]), jnp.concatenate(wide[half:])]
    early_keys = after(early_keys, wide[-2])
    far_half = [swap(unit, "seq", 1) for unit in near_half]

    summed = both_gradients(
        place, early_keys, early_values, early_rates, fast, acc, outer, grad_scale
    )
    arrived = [swap(summed[step], "seq", step * 2) for step in range(1, outer)]
    arrived[0] = after(arrived[0], far_half[0])
    total = summed[0]
    for piece in arrived:
        total = total + piece.astype(jnp.float32)
    moment_own = MOMENTUM_DECAY * momentum[0] + total
    base_rows = lax.dynamic_slice_in_dim(fast[0], position * own_rows, own_rows, 1).astype(jnp.float32)
    near = [renormalize(base_rows, moment_own)]
    far = [swap(near[0], "seq", 1)]
    for step in range(1, outer):
        near.append(ring_step(near[-1], outer))
        if step == 2:
            near[-1] = after(near[-1], far_half[1])
        if step > 1:
            near[-1] = after(near[-1], far[step - 2])
        far.append(swap(near[-1], "seq", 1))

    attended = attention(queries, keys, values, early_keys, early_values, position)
    combined = apply_fast(origins, queries, attended, near + far)

    blocks = [(combined, 0)]
    mask = heads // 2
    while mask:
        blocks = blocks + [(swap(block, "head", mask), tag ^ mask) for block, tag in blocks]
        mask //= 2
    origins = jnp.concatenate([origins, head[None].astype(jnp.int32)])
    early = [pair for pair in blocks if pair[1] <= 1]
    late = [pair for pair in blocks if pair[1] > 1]
    mixed = None
    for group in (early, late):
        mixed = project(
            origins, [b for b, _ in group], [t for _, t in group], near_half + far_half, mixed
        )
    return (mixed, moment_own[None])


def plain(queries, keys, values, rates, fast, momentum, out_proj):
    tok_rows = queries.shape[0]
    ranks = lax.axis_size("seq")
    position = lax.axis_index("seq")
    own_rows = momentum.shape[2]
    grad_scale = 1.0 / math.sqrt(tok_rows * ranks)
    weights = fast[0]
    h_gate = times_transposed(keys, weights[0])
    h_up = times_transposed(keys, weights[1])
    sigma = jax.nn.sigmoid(h_gate)
    gated = (h_gate * sigma * h_up).astype(jnp.bfloat16)
    errors = (-grad_scale * rates * values.astype(jnp.float32)).astype(jnp.bfloat16)
    grad_down = contract_rows(errors, gated)
    back = matmul(errors, weights[2])
    d_gate = (back * h_up * sigma * (1.0 + h_gate * (1.0 - sigma))).astype(jnp.bfloat16)
    d_up = (back * h_gate * sigma).astype(jnp.bfloat16)
    grads = jnp.stack([contract_rows(d_gate, keys), contract_rows(d_up, keys), grad_down])
    summed_rows = lax.psum_scatter(grads, "seq", scatter_dimension=1, tiled=True)
    moment_own = MOMENTUM_DECAY * momentum[0] + summed_rows
    base_rows = lax.dynamic_slice_in_dim(weights, position * own_rows, own_rows, 1).astype(jnp.float32)
    renewed = lax.all_gather(renormalize(base_rows, moment_own), "seq", axis=1, tiled=True)
    q_gate = times_transposed(queries, renewed[0])
    q_up = times_transposed(queries, renewed[1])
    fast_in = (q_gate * jax.nn.sigmoid(q_gate) * q_up).astype(jnp.bfloat16)
    fast_out = times_transposed(fast_in, renewed[2])
    behind = [(i, i + 1) for i in range(ranks - 1)]
    early_keys = lax.ppermute(keys, "seq", behind)
    early_values = lax.ppermute(values, "seq", behind)
    attended = attention(queries, keys, values, early_keys, early_values, position)
    combined = (attended + fast_out).astype(jnp.bfloat16)
    all_heads = lax.all_gather(combined, "head", axis=1, tiled=True)
    projection = lax.all_gather(out_proj, "seq", axis=0, tiled=True)
    return (matmul(all_heads, projection).astype(jnp.bfloat16), moment_own[None])


def solution(mesh):
    return jax.shard_map(
        shards,
        mesh=mesh,
        in_specs=(
            P("seq", "head"),
            P("seq", "head"),
            P("seq", "head"),
            P("seq", "head"),
            P("head", None, None, None),
            P("head", None, "seq", None),
            P("seq", "head"),
        ),
        out_specs=(P("seq", "head"), P("head", None, "seq", None)),
        check_vma=False,
    )
```

profile of v0, /device:TPU:0, one launch (start us, length us, event | category | flops | bytes accessed | tf_op | source)
XLA Modules:
  0.0 124.3 jit_solution(15049809767448327736)
XLA Ops:
  0.7 1.4 %copy-done.1 = bf16[1,3,512,512]{3,2,1,0:T(8,128)(2,1)S(1)} copy-done((bf16[1,3,512,512]{3,2,1,0:T(8,128)(2,1)S(1)}, bf16[1,3,512,512]{3,2,1,0:T(8,128)(2,1)}, u32[]{:S(2)}) %copy-start.1) | copy-done | bytes 1572888
  2.1 3.5 %own_gradients.1.acc = f32[4,3,64,512]{3,2,1,0:T(8,128)S(1)} custom-call(s32[2]{0:T(128)S(1)} %pad_add_fusion.1.place, bf16[512,512]{1,0:T(8,128)(2,1)} %k.1, bf16[512,512]{1,0:T(8,128)(2,1)} %v.1, f32[1,512]{1,0:T(1,128)} %bitcast.4.r, bf16[1,3,512,512]{3,2,1,0:T(8,128)(2,1)S(1)} %copy-done.1), custom_call_target="tpu_custom_call" | custom-call | flops 1610612736 | bytes 4000000 | tf_op jit(solution)/shard_map/own_gradients/pallas_call | solution.py:127
  6.8 3.0 %collective-permute-start.1 = (bf16[256,512]{1,0:T(8,128)(2,1)S(1)}, bf16[256,512]{1,0:T(8,128)(2,1)S(1)}, u32[]{:S(2)}, u32[]{:S(2)}) collective-permute-start(bf16[256,512]{1,0:T(8,128)(2,1)S(1)} %copy-done.9), channel_id=1, source_target_pairs={{0,8},{4,12},{8,24},{12,28},{24,16},{28,20},{16,0},{20,4},{1,9},{5... | collective-permute-start | bytes 786440 | tf_op jit(solution)/shard_map/ppermute | solution.py:235
  9.9 1.5 %collective-permute-start = (bf16[512,512]{1,0:T(8,128)(2,1)}, bf16[512,512]{1,0:T(8,128)(2,1)}, u32[]{:S(2)}, u32[]{:S(2)}) collective-permute-start(bf16[512,512]{1,0:T(8,128)(2,1)} %k.1), channel_id=1, source_target_pairs={{0,4},{4,8},{8,12},{12,16},{16,20},{20,24},{24,28},{28,0},{1,5},{5... | collective-permute-start | bytes 1572872 | tf_op jit(solution)/shard_map/ppermute | solution.py:291
  11.4 2.5 %collective-permute-start.3 = (bf16[512,512]{1,0:T(8,128)(2,1)}, bf16[512,512]{1,0:T(8,128)(2,1)S(1)}, u32[]{:S(2)}, u32[]{:S(2)}) collective-permute-start(bf16[512,512]{1,0:T(8,128)(2,1)} %v.1), channel_id=1, source_target_pairs={{0,4},{4,8},{8,12},{12,16},{16,20},{20,24},{24,28},{28,0},{1,5},{5... | collective-permute-start | bytes 1572872 | tf_op jit(solution)/shard_map/ppermute | solution.py:292
  13.9 3.3 %collective-permute-done.1 = bf16[256,512]{1,0:T(8,128)(2,1)S(1)} collective-permute-done((bf16[256,512]{1,0:T(8,128)(2,1)S(1)}, bf16[256,512]{1,0:T(8,128)(2,1)S(1)}, u32[]{:S(2)}, u32[]{:S(2)}) %collective-permute-start.1) | collective-permute-done | bytes 262176 | tf_op jit(solution)/shard_map/ppermute | solution.py:235
  18.0 2.7 %collective-permute-start.6 = (bf16[512,512]{1,0:T(8,128)(2,1)S(1)}, bf16[512,512]{1,0:T(8,128)(2,1)S(1)}, u32[]{:S(2)}, u32[]{:S(2)}) collective-permute-start(bf16[512,512]{1,0:T(8,128)(2,1)S(1)} %constant_dynamic-update-slice_fusion.rest_2_), channel_id=1, source_target_pairs={{0,4},{4,0},{8,12},{12,8},{16,20},{20,16},{24,28},{28,24},{1,5},{5... | collective-permute-start | bytes 1572872 | tf_op jit(solution)/shard_map/ppermute | solution.py:39
  20.9 11.1 %collective-permute-done.k = bf16[512,512]{1,0:T(8,128)(2,1)} collective-permute-done((bf16[512,512]{1,0:T(8,128)(2,1)}, bf16[512,512]{1,0:T(8,128)(2,1)}, u32[]{:S(2)}, u32[]{:S(2)}) %collective-permute-start) | collective-permute-done | bytes 524320 | tf_op jit(solution)/shard_map/ppermute | solution.py:291
  31.9 15.6 %collective-permute-done.4.r = f32[1,512]{1,0:T(1,128)S(1)} collective-permute-done((f32[1,512]{1,0:T(1,128)}, f32[1,512]{1,0:T(1,128)S(1)}, u32[]{:S(2)}, u32[]{:S(2)}) %collective-permute-start.4) | collective-permute-done | bytes 2080 | tf_op jit(solution)/shard_map/ppermute | solution.py:293
  47.6 1.4 %copy-done.6 = f32[4,3,64,512]{3,2,1,0:T(8,128)S(1)} copy-done((f32[4,3,64,512]{3,2,1,0:T(8,128)S(1)}, f32[4,3,64,512]{3,2,1,0:T(8,128)}, u32[]{:S(2)}) %copy-start.6) | copy-done | bytes 1572888
  49.0 3.5 %both_gradients.1 = (f32[3,64,512]{2,1,0:T(8,128)S(1)}, bf16[3,64,512]{2,1,0:T(8,128)(2,1)S(1)}, bf16[3,64,512]{2,1,0:T(8,128)(2,1)S(1)}, bf16[3,64,512]{2,1,0:T(8,128)(2,1)S(1)}) custom-call(s32[2]{0:T(128)S(1)} %pad_add_fusion.1.place, bf16[512,512]{1,0:T(8,128)(2,1)} %collective-permute-done.k, bf16[512,512]{1,0:T(8,128)(2,1)S(1)} %collective-permute-done.3.v, ...), custom_call_target="tpu_custom_call" | custom-call | flops 1610612736 | bytes 4000000 | tf_op jit(solution)/shard_map/both_gradients/pallas_call | solution.py:142
  52.6 1.7 %collective-permute-start.7 = (bf16[3,64,512]{2,1,0:T(8,128)(2,1)S(1)}, bf16[3,64,512]{2,1,0:T(8,128)(2,1)S(1)}, u32[]{:S(2)}, u32[]{:S(2)}) collective-permute-start(bf16[3,64,512]{2,1,0:T(8,128)(2,1)S(1)} %get-tuple-element.17), channel_id=1, source_target_pairs={{0,16},{4,20},{8,24},{12,28},{16,0},{20,4},{24,8},{28,12},{1,17},{... | collective-permute-start | bytes 589832 | tf_op jit(solution)/shard_map/ppermute | solution.py:39
  54.3 2.7 %collective-permute-start.5 = (bf16[3,64,512]{2,1,0:T(8,128)(2,1)S(1)}, bf16[3,64,512]{2,1,0:T(8,128)(2,1)S(1)}, u32[]{:S(2)}, u32[]{:S(2)}) collective-permute-start(bf16[3,64,512]{2,1,0:T(8,128)(2,1)S(1)} %get-tuple-element.15), channel_id=1, source_target_pairs={{0,8},{4,12},{8,0},{12,4},{16,24},{20,28},{24,16},{28,20},{1,9},{5... | collective-permute-start | bytes 589832 | tf_op jit(solution)/shard_map/ppermute | solution.py:39
  58.0 8.4 %collective-permute-done.5 = bf16[3,64,512]{2,1,0:T(8,128)(2,1)S(1)} collective-permute-done((bf16[3,64,512]{2,1,0:T(8,128)(2,1)S(1)}, bf16[3,64,512]{2,1,0:T(8,128)(2,1)S(1)}, u32[]{:S(2)}, u32[]{:S(2)}) %collective-permute-start.5) | collective-permute-done | bytes 196640 | tf_op jit(solution)/shard_map/ppermute | solution.py:39
  66.4 6.1 %collective-permute-done.7 = bf16[3,64,512]{2,1,0:T(8,128)(2,1)S(1)} collective-permute-done((bf16[3,64,512]{2,1,0:T(8,128)(2,1)S(1)}, bf16[3,64,512]{2,1,0:T(8,128)(2,1)S(1)}, u32[]{:S(2)}, u32[]{:S(2)}) %collective-permute-start.7) | collective-permute-done | bytes 196640 | tf_op jit(solution)/shard_map/ppermute | solution.py:39
  73.0 5.1 %collective-permute-done.11 = bf16[256,512]{1,0:T(8,128)(2,1)S(1)} collective-permute-done((bf16[256,512]{1,0:T(8,128)(2,1)}, bf16[256,512]{1,0:T(8,128)(2,1)S(1)}, u32[]{:S(2)}, u32[]{:S(2)}) %collective-permute-start.11) | collective-permute-done | bytes 262176 | tf_op jit(solution)/shard_map/ppermute | solution.py:235
  78.2 2.0 %collective-permute-start.12 = (bf16[512,512]{1,0:T(8,128)(2,1)S(1)}, bf16[512,512]{1,0:T(8,128)(2,1)S(1)}, u32[]{:S(2)}, u32[]{:S(2)}) collective-permute-start(bf16[512,512]{1,0:T(8,128)(2,1)S(1)} %constant_dynamic-update-slice_fusion.2.rest_3_), channel_id=1, source_target_pairs={{0,4},{4,0},{8,12},{12,8},{16,20},{20,16},{24,28},{28,24},{1,5},{5... | collective-permute-start | bytes 1572872 | tf_op jit(solution)/shard_map/ppermute | solution.py:39
  81.0 2.6 %fusion.14 = (f32[512]{0:T(512)S(1)}, f32[512,1024]{0,1:T(8,128)S(1)}) fusion(bf16[512,512]{1,0:T(8,128)(2,1)S(1)} %copy-done, bf16[512,512]{1,0:T(8,128)(2,1)} %k.1, bf16[512,512]{1,0:T(8,128)(2,1)} %collective-permute-done.k, pred[1024]{0:T(1024)(128)(4,1)S(1)} %broadcast_compare_fusion, s32[1024]{0:T(1024)S(1)} %iota_add_fusion, s32[512]{0:T(512)S(1)} %iota_add_fusion.1), kind=kOutput, calls=%fused_computation.35 | convolution fusion | flops 543161856 | bytes 3679232 | tf_op jit(solution)/shard_map/dot_general | solution.py:22
  83.6 2.0 %collective-permute-start.15 = (bf16[3,64,512]{2,1,0:T(8,128)(2,1)S(1)}, bf16[3,64,512]{2,1,0:T(8,128)(2,1)S(1)}, u32[]{:S(2)}, u32[]{:S(2)}) collective-permute-start(bf16[3,64,512]{2,1,0:T(8,128)(2,1)S(1)} %collective-permute-done.9.rest_1_), channel_id=1, source_target_pairs={{0,4},{4,0},{8,12},{12,8},{16,20},{20,16},{24,28},{28,24},{1,5},{5... | collective-permute-start | bytes 589832 | tf_op jit(solution)/shard_map/ppermute | solution.py:39
  85.7 1.9 %collective-permute-done.10.rest_2_ = bf16[3,64,512]{2,1,0:T(8,128)(2,1)S(1)} collective-permute-done((bf16[3,64,512]{2,1,0:T(8,128)(2,1)S(1)}, bf16[3,64,512]{2,1,0:T(8,128)(2,1)S(1)}, u32[]{:S(2)}, u32[]{:S(2)}) %collective-permute-start.10) | collective-permute-done | bytes 196640 | tf_op jit(solution)/shard_map/ppermute | solution.py:235
  87.5 5.2 %collective-permute-done.12.rest_5_ = bf16[512,512]{1,0:T(8,128)(2,1)S(1)} collective-permute-done((bf16[512,512]{1,0:T(8,128)(2,1)S(1)}, bf16[512,512]{1,0:T(8,128)(2,1)S(1)}, u32[]{:S(2)}, u32[]{:S(2)}) %collective-permute-start.12) | collective-permute-done | bytes 524320 | tf_op jit(solution)/shard_map/ppermute | solution.py:39
  92.8 3.2 %collective-permute-done.13.rest_4_ = bf16[3,64,512]{2,1,0:T(8,128)(2,1)S(1)} collective-permute-done((bf16[3,64,512]{2,1,0:T(8,128)(2,1)S(1)}, bf16[3,64,512]{2,1,0:T(8,128)(2,1)S(1)}, u32[]{:S(2)}, u32[]{:S(2)}) %collective-permute-start.13) | collective-permute-done | bytes 196640 | tf_op jit(solution)/shard_map/ppermute | solution.py:39
  96.3 2.5 %collective-permute-start.16 = (bf16[3,64,512]{2,1,0:T(8,128)(2,1)S(1)}, bf16[3,64,512]{2,1,0:T(8,128)(2,1)S(1)}, u32[]{:S(2)}, u32[]{:S(2)}) collective-permute-start(bf16[3,64,512]{2,1,0:T(8,128)(2,1)S(1)} %collective-permute-done.10.rest_2_), channel_id=1, source_target_pairs={{0,4},{4,0},{8,12},{12,8},{16,20},{20,16},{24,28},{28,24},{1,5},{5... | collective-permute-start | bytes 589832 | tf_op jit(solution)/shard_map/ppermute | solution.py:39
  100.2 2.4 %collective-permute-done.14.rest_3_ = bf16[3,64,512]{2,1,0:T(8,128)(2,1)S(1)} collective-permute-done((bf16[3,64,512]{2,1,0:T(8,128)(2,1)S(1)}, bf16[3,64,512]{2,1,0:T(8,128)(2,1)S(1)}, u32[]{:S(2)}, u32[]{:S(2)}) %collective-permute-start.14) | collective-permute-done | bytes 196640 | tf_op jit(solution)/shard_map/ppermute | solution.py:235
  102.5 2.5 %collective-permute-start.17 = (bf16[3,64,512]{2,1,0:T(8,128)(2,1)S(1)}, bf16[3,64,512]{2,1,0:T(8,128)(2,1)S(1)}, u32[]{:S(2)}, u32[]{:S(2)}) collective-permute-start(bf16[3,64,512]{2,1,0:T(8,128)(2,1)S(1)} %collective-permute-done.14.rest_3_), channel_id=1, source_target_pairs={{0,4},{4,0},{8,12},{12,8},{16,20},{20,16},{24,28},{28,24},{1,5},{5... | collective-permute-start | bytes 589832 | tf_op jit(solution)/shard_map/ppermute | solution.py:39
  105.0 1.8 %fusion.6.attended = f32[512,512]{1,0:T(8,128)S(1)} fusion(bf16[512,512]{1,0:T(8,128)(2,1)} %v.1, bf16[512,512]{1,0:T(8,128)(2,1)S(1)} %copy-done.4, f32[512,1024]{0,1:T(8,128)S(1)} %get-tuple-element.26, f32[512]{0:T(512)S(1)} %fusion.2, f32[512]{0:T(512)S(1)} %get-tuple-element.25), kind=kOutput, calls=%fused_computation.11 | convolution fusion | flops 540540928 | bytes 4198400 | tf_op jit(solution)/shard_map/dot_general | solution.py:272
  106.8 1.8 %collective-permute-done.17.rest_7_ = bf16[3,64,512]{2,1,0:T(8,128)(2,1)S(1)} collective-permute-done((bf16[3,64,512]{2,1,0:T(8,128)(2,1)S(1)}, bf16[3,64,512]{2,1,0:T(8,128)(2,1)S(1)}, u32[]{:S(2)}, u32[]{:S(2)}) %collective-permute-start.17) | collective-permute-done | bytes 196640 | tf_op jit(solution)/shard_map/ppermute | solution.py:39
  108.6 1.7 %apply_fast.1.rest_0_ = bf16[512,512]{1,0:T(8,128)(2,1)S(1)} custom-call(s32[8]{0:T(128)S(1)} %dynamic-slice_bitcast_fusion.origin, bf16[512,512]{1,0:T(8,128)(2,1)S(1)} %copy-done, f32[512,512]{1,0:T(8,128)S(1)} %fusion.6.attended, bf16[3,64,512]{2,1,0:T(8,128)(2,1)S(1)} %multiply_convert_fusion.rest_0_, ...), custom_call_target="tpu_custom_call" | custom-call | flops 805306368 | bytes 4000000 | tf_op jit(solution)/shard_map/apply_fast/pallas_call | solution.py:170
  110.3 1.6 %collective-permute-start.18 = (bf16[512,512]{1,0:T(8,128)(2,1)S(1)}, bf16[512,512]{1,0:T(8,128)(2,1)S(1)}, u32[]{:S(2)}, u32[]{:S(2)}) collective-permute-start(bf16[512,512]{1,0:T(8,128)(2,1)S(1)} %apply_fast.1.rest_0_), channel_id=1, source_target_pairs={{0,2},{1,3},{2,0},{3,1},{4,6},{5,7},{6,4},{7,5},{8,10},{9,11},{10,... | collective-permute-start | bytes 1572872 | tf_op jit(solution)/shard_map/ppermute | solution.py:39
  111.9 7.6 %collective-permute-done.18.rest_0_ = bf16[512,512]{1,0:T(8,128)(2,1)S(1)} collective-permute-done((bf16[512,512]{1,0:T(8,128)(2,1)S(1)}, bf16[512,512]{1,0:T(8,128)(2,1)S(1)}, u32[]{:S(2)}, u32[]{:S(2)}) %collective-permute-start.18) | collective-permute-done | bytes 524320 | tf_op jit(solution)/shard_map/ppermute | solution.py:39
  119.6 1.9 %project.2.rest_6_ = f32[512,512]{1,0:T(8,128)S(1)} custom-call(s32[9]{0:T(128)S(1)} %pad_add_fusion.origin, bf16[512,512]{1,0:T(8,128)(2,1)S(1)} %apply_fast.1.rest_0_, bf16[512,512]{1,0:T(8,128)(2,1)} %collective-permute-done.20.rest_1_, bf16[512,512]{1,0:T(8,128)(2,1)S(1)} %constant_dynamic-update-slice_fusion.rest_2_, ...), custom_call_target="tpu_custom_call" | custom-call | flops 536870912 | bytes 4000000 | tf_op jit(solution)/shard_map/project/pallas_call | solution.py:208
  121.6 2.7 %project.3 = bf16[512,512]{1,0:T(8,128)(2,1)} custom-call(s32[9]{0:T(128)S(1)} %pad_add_fusion.origin, bf16[512,512]{1,0:T(8,128)(2,1)S(1)} %collective-permute-done.18.rest_0_, bf16[512,512]{1,0:T(8,128)(2,1)} %collective-permute-done.19.rest_1_, bf16[512,512]{1,0:T(8,128)(2,1)S(1)} %constant_dynamic-update-slice_fusion.rest_2_, ...), custom_call_target="tpu_custom_call" | custom-call | flops 536870912 | bytes 4000000 | tf_op jit(solution)/shard_map/project/pallas_call | solution.py:208
  (51 shorter events, 6.4 us)
Async XLA Ops:
  0.7 1.4 %copy-start.1 = (bf16[1,3,512,512]{3,2,1,0:T(8,128)(2,1)S(1)}, bf16[1,3,512,512]{3,2,1,0:T(8,128)(2,1)}, u32[]{:S(2)}) copy-start(bf16[1,3,512,512]{3,2,1,0:T(8,128)(2,1)} %w.3) | copy-start | bytes 4718596
  2.1 4.7 %copy-start.9 = (bf16[256,512]{1,0:T(8,128)(2,1)S(1)}, bf16[256,512]{1,0:T(8,128)(2,1)}, u32[]{:S(2)}) copy-start(bf16[256,512]{1,0:T(8,128)(2,1)} %param.14) | copy-start | bytes 786436
  2.1 45.4 %copy-start.2 = (bf16[1,3,512,512]{3,2,1,0:T(8,128)(2,1)S(1)}, bf16[1,3,512,512]{3,2,1,0:T(8,128)(2,1)}, u32[]{:S(2)}) copy-start(bf16[1,3,512,512]{3,2,1,0:T(8,128)(2,1)} %w.3) | copy-start | bytes 4718596
  5.7 1.2 copy-start.5
  6.8 10.3 %collective-permute-start.1 = (bf16[256,512]{1,0:T(8,128)(2,1)S(1)}, bf16[256,512]{1,0:T(8,128)(2,1)S(1)}, u32[]{:S(2)}, u32[]{:S(2)}) collective-permute-start(bf16[256,512]{1,0:T(8,128)(2,1)S(1)} %copy-done.9), channel_id=1, source_target_pairs={{0,8},{4,12},{8,24},{12,28},{24,16},{28,20},{16,0},{20,4},{1,9},{5... | collective-permute-start | bytes 786440 | tf_op jit(solution)/shard_map/ppermute | solution.py:235
  9.9 22.1 %collective-permute-start = (bf16[512,512]{1,0:T(8,128)(2,1)}, bf16[512,512]{1,0:T(8,128)(2,1)}, u32[]{:S(2)}, u32[]{:S(2)}) collective-permute-start(bf16[512,512]{1,0:T(8,128)(2,1)} %k.1), channel_id=1, source_target_pairs={{0,4},{4,8},{8,12},{12,16},{16,20},{20,24},{24,28},{28,0},{1,5},{5... | collective-permute-start | bytes 1572872 | tf_op jit(solution)/shard_map/ppermute | solution.py:291
  11.4 36.2 %collective-permute-start.3 = (bf16[512,512]{1,0:T(8,128)(2,1)}, bf16[512,512]{1,0:T(8,128)(2,1)S(1)}, u32[]{:S(2)}, u32[]{:S(2)}) collective-permute-start(bf16[512,512]{1,0:T(8,128)(2,1)} %v.1), channel_id=1, source_target_pairs={{0,4},{4,8},{8,12},{12,16},{16,20},{20,24},{24,28},{28,0},{1,5},{5... | collective-permute-start | bytes 1572872 | tf_op jit(solution)/shard_map/ppermute | solution.py:292
  17.2 14.8 %collective-permute-start.2 = (bf16[256,512]{1,0:T(8,128)(2,1)S(1)}, bf16[256,512]{1,0:T(8,128)(2,1)}, u32[]{:S(2)}, u32[]{:S(2)}) collective-permute-start(bf16[256,512]{1,0:T(8,128)(2,1)S(1)} %collective-permute-done.1), channel_id=1, source_target_pairs={{0,8},{4,12},{8,24},{12,28},{24,16},{28,20},{16,0},{20,4},{1,9},{5... | collective-permute-start | bytes 786440 | tf_op jit(solution)/shard_map/ppermute | solution.py:235
  18.0 48.4 %collective-permute-start.6 = (bf16[512,512]{1,0:T(8,128)(2,1)S(1)}, bf16[512,512]{1,0:T(8,128)(2,1)S(1)}, u32[]{:S(2)}, u32[]{:S(2)}) collective-permute-start(bf16[512,512]{1,0:T(8,128)(2,1)S(1)} %constant_dynamic-update-slice_fusion.rest_2_), channel_id=1, source_target_pairs={{0,4},{4,0},{8,12},{12,8},{16,20},{20,16},{24,28},{28,24},{1,5},{5... | collective-permute-start | bytes 1572872 | tf_op jit(solution)/shard_map/ppermute | solution.py:39
  20.8 26.8 %collective-permute-start.4 = (f32[1,512]{1,0:T(1,128)}, f32[1,512]{1,0:T(1,128)S(1)}, u32[]{:S(2)}, u32[]{:S(2)}) collective-permute-start(f32[1,512]{1,0:T(1,128)} %bitcast.4.r), channel_id=1, source_target_pairs={{0,4},{4,8},{8,12},{12,16},{16,20},{20,24},{24,28},{28,0},{1,5},{5... | collective-permute-start | bytes 6152 | tf_op jit(solution)/shard_map/ppermute | solution.py:293
  47.6 1.4 %copy-start.6 = (f32[4,3,64,512]{3,2,1,0:T(8,128)S(1)}, f32[4,3,64,512]{3,2,1,0:T(8,128)}, u32[]{:S(2)}) copy-start(f32[4,3,64,512]{3,2,1,0:T(8,128)} %copy-done.5) | copy-start | bytes 4718596
  49.0 3.5 %copy-start.3 = (bf16[512,512]{1,0:T(8,128)(2,1)}, bf16[512,512]{1,0:T(8,128)(2,1)S(1)}, u32[]{:S(2)}) copy-start(bf16[512,512]{1,0:T(8,128)(2,1)S(1)} %collective-permute-done.3.v) | copy-start | bytes 1572868
  49.0 23.6 %copy-start.8 = (f32[1,3,64,512]{3,2,1,0:T(8,128)S(1)}, f32[1,3,64,512]{3,2,1,0:T(8,128)}, u32[]{:S(2)}) copy-start(f32[1,3,64,512]{3,2,1,0:T(8,128)} %param.13) | copy-start | bytes 1179652
  52.5 28.5 %copy-start = (bf16[512,512]{1,0:T(8,128)(2,1)S(1)}, bf16[512,512]{1,0:T(8,128)(2,1)}, u32[]{:S(2)}) copy-start(bf16[512,512]{1,0:T(8,128)(2,1)} %q.1) | copy-start | bytes 1572868
  52.5 13.9 %collective-permute-start.8 = (bf16[3,64,512]{2,1,0:T(8,128)(2,1)S(1)}, bf16[3,64,512]{2,1,0:T(8,128)(2,1)S(1)}, u32[]{:S(2)}, u32[]{:S(2)}) collective-permute-start(bf16[3,64,512]{2,1,0:T(8,128)(2,1)S(1)} %get-tuple-element.18), channel_id=1, source_target_pairs={{0,24},{4,28},{8,16},{12,20},{16,8},{20,12},{24,0},{28,4},{1,25},{... | collective-permute-start | bytes 589832 | tf_op jit(solution)/shard_map/ppermute | solution.py:39
  52.6 20.0 %collective-permute-start.7 = (bf16[3,64,512]{2,1,0:T(8,128)(2,1)S(1)}, bf16[3,64,512]{2,1,0:T(8,128)(2,1)S(1)}, u32[]{:S(2)}, u32[]{:S(2)}) collective-permute-start(bf16[3,64,512]{2,1,0:T(8,128)(2,1)S(1)} %get-tuple-element.17), channel_id=1, source_target_pairs={{0,16},{4,20},{8,24},{12,28},{16,0},{20,4},{24,8},{28,12},{1,17},{... | collective-permute-start | bytes 589832 | tf_op jit(solution)/shard_map/ppermute | solution.py:39
  54.3 12.1 %collective-permute-start.5 = (bf16[3,64,512]{2,1,0:T(8,128)(2,1)S(1)}, bf16[3,64,512]{2,1,0:T(8,128)(2,1)S(1)}, u32[]{:S(2)}, u32[]{:S(2)}) collective-permute-start(bf16[3,64,512]{2,1,0:T(8,128)(2,1)S(1)} %get-tuple-element.15), channel_id=1, source_target_pairs={{0,8},{4,12},{8,0},{12,4},{16,24},{20,28},{24,16},{28,20},{1,9},{5... | collective-permute-start | bytes 589832 | tf_op jit(solution)/shard_map/ppermute | solution.py:39
  57.0 21.2 %collective-permute-start.11 = (bf16[256,512]{1,0:T(8,128)(2,1)}, bf16[256,512]{1,0:T(8,128)(2,1)S(1)}, u32[]{:S(2)}, u32[]{:S(2)}) collective-permute-start(bf16[256,512]{1,0:T(8,128)(2,1)} %collective-permute-done.2), channel_id=1, source_target_pairs={{0,8},{4,12},{8,24},{12,28},{24,16},{28,20},{16,0},{20,4},{1,9},{5... | collective-permute-start | bytes 786440 | tf_op jit(solution)/shard_map/ppermute | solution.py:235
  72.8 10.8 %copy-start.7 = (f32[3,64,512]{2,1,0:T(8,128)}, f32[3,64,512]{2,1,0:T(8,128)S(1)}, u32[]{:S(2)}) copy-start(f32[3,64,512]{2,1,0:T(8,128)S(1)} %get-tuple-element.24) | copy-start | bytes 1179652
  73.0 8.0 %collective-permute-start.9 = (bf16[3,64,512]{2,1,0:T(8,128)(2,1)S(1)}, bf16[3,64,512]{2,1,0:T(8,128)(2,1)S(1)}, u32[]{:S(2)}, u32[]{:S(2)}) collective-permute-start(bf16[3,64,512]{2,1,0:T(8,128)(2,1)S(1)} %multiply_convert_fusion.rest_0_), channel_id=1, source_target_pairs={{0,8},{4,12},{8,24},{12,28},{24,16},{28,20},{16,0},{20,4},{1,9},{5... | collective-permute-start | bytes 589832 | tf_op jit(solution)/shard_map/ppermute | solution.py:235
  78.2 14.6 %collective-permute-start.12 = (bf16[512,512]{1,0:T(8,128)(2,1)S(1)}, bf16[512,512]{1,0:T(8,128)(2,1)S(1)}, u32[]{:S(2)}, u32[]{:S(2)}) collective-permute-start(bf16[512,512]{1,0:T(8,128)(2,1)S(1)} %constant_dynamic-update-slice_fusion.2.rest_3_), channel_id=1, source_target_pairs={{0,4},{4,0},{8,12},{12,8},{16,20},{20,16},{24,28},{28,24},{1,5},{5... | collective-permute-start | bytes 1572872 | tf_op jit(solution)/shard_map/ppermute | solution.py:39
  80.9 15.0 %collective-permute-start.13 = (bf16[3,64,512]{2,1,0:T(8,128)(2,1)S(1)}, bf16[3,64,512]{2,1,0:T(8,128)(2,1)S(1)}, u32[]{:S(2)}, u32[]{:S(2)}) collective-permute-start(bf16[3,64,512]{2,1,0:T(8,128)(2,1)S(1)} %multiply_convert_fusion.rest_0_), channel_id=1, source_target_pairs={{0,4},{4,0},{8,12},{12,8},{16,20},{20,16},{24,28},{28,24},{1,5},{5... | collective-permute-start | bytes 589832 | tf_op jit(solution)/shard_map/ppermute | solution.py:39
  81.0 6.6 %collective-permute-start.10 = (bf16[3,64,512]{2,1,0:T(8,128)(2,1)S(1)}, bf16[3,64,512]{2,1,0:T(8,128)(2,1)S(1)}, u32[]{:S(2)}, u32[]{:S(2)}) collective-permute-start(bf16[3,64,512]{2,1,0:T(8,128)(2,1)S(1)} %collective-permute-done.9.rest_1_), channel_id=1, source_target_pairs={{0,8},{4,12},{8,24},{12,28},{24,16},{28,20},{16,0},{20,4},{1,9},{5... | collective-permute-start | bytes 589832 | tf_op jit(solution)/shard_map/ppermute | solution.py:235
  83.6 21.4 %copy-start.4 = (bf16[512,512]{1,0:T(8,128)(2,1)S(1)}, bf16[512,512]{1,0:T(8,128)(2,1)}, u32[]{:S(2)}) copy-start(bf16[512,512]{1,0:T(8,128)(2,1)} %copy-done.3) | copy-start | bytes 1572868
  83.6 16.5 %collective-permute-start.15 = (bf16[3,64,512]{2,1,0:T(8,128)(2,1)S(1)}, bf16[3,64,512]{2,1,0:T(8,128)(2,1)S(1)}, u32[]{:S(2)}, u32[]{:S(2)}) collective-permute-start(bf16[3,64,512]{2,1,0:T(8,128)(2,1)S(1)} %collective-permute-done.9.rest_1_), channel_id=1, source_target_pairs={{0,4},{4,0},{8,12},{12,8},{16,20},{20,16},{24,28},{28,24},{1,5},{5... | collective-permute-start | bytes 589832 | tf_op jit(solution)/shard_map/ppermute | solution.py:39
  95.9 6.6 %collective-permute-start.14 = (bf16[3,64,512]{2,1,0:T(8,128)(2,1)S(1)}, bf16[3,64,512]{2,1,0:T(8,128)(2,1)S(1)}, u32[]{:S(2)}, u32[]{:S(2)}) collective-permute-start(bf16[3,64,512]{2,1,0:T(8,128)(2,1)S(1)} %collective-permute-done.10.rest_2_), channel_id=1, source_target_pairs={{0,8},{4,12},{8,24},{12,28},{24,16},{28,20},{16,0},{20,4},{1,9},{5... | collective-permute-start | bytes 589832 | tf_op jit(solution)/shard_map/ppermute | solution.py:235
  96.3 10.5 %collective-permute-start.16 = (bf16[3,64,512]{2,1,0:T(8,128)(2,1)S(1)}, bf16[3,64,512]{2,1,0:T(8,128)(2,1)S(1)}, u32[]{:S(2)}, u32[]{:S(2)}) collective-permute-start(bf16[3,64,512]{2,1,0:T(8,128)(2,1)S(1)} %collective-permute-done.10.rest_2_), channel_id=1, source_target_pairs={{0,4},{4,0},{8,12},{12,8},{16,20},{20,16},{24,28},{28,24},{1,5},{5... | collective-permute-start | bytes 589832 | tf_op jit(solution)/shard_map/ppermute | solution.py:39
  102.5 6.1 %collective-permute-start.17 = (bf16[3,64,512]{2,1,0:T(8,128)(2,1)S(1)}, bf16[3,64,512]{2,1,0:T(8,128)(2,1)S(1)}, u32[]{:S(2)}, u32[]{:S(2)}) collective-permute-start(bf16[3,64,512]{2,1,0:T(8,128)(2,1)S(1)} %collective-permute-done.14.rest_3_), channel_id=1, source_target_pairs={{0,4},{4,0},{8,12},{12,8},{16,20},{20,16},{24,28},{28,24},{1,5},{5... | collective-permute-start | bytes 589832 | tf_op jit(solution)/shard_map/ppermute | solution.py:39
  110.3 9.2 %collective-permute-start.18 = (bf16[512,512]{1,0:T(8,128)(2,1)S(1)}, bf16[512,512]{1,0:T(8,128)(2,1)S(1)}, u32[]{:S(2)}, u32[]{:S(2)}) collective-permute-start(bf16[512,512]{1,0:T(8,128)(2,1)S(1)} %apply_fast.1.rest_0_), channel_id=1, source_target_pairs={{0,2},{1,3},{2,0},{3,1},{4,6},{5,7},{6,4},{7,5},{8,10},{9,11},{10,... | collective-permute-start | bytes 1572872 | tf_op jit(solution)/shard_map/ppermute | solution.py:39
  111.9 7.7 %collective-permute-start.20 = (bf16[512,512]{1,0:T(8,128)(2,1)S(1)}, bf16[512,512]{1,0:T(8,128)(2,1)}, u32[]{:S(2)}, u32[]{:S(2)}) collective-permute-start(bf16[512,512]{1,0:T(8,128)(2,1)S(1)} %apply_fast.1.rest_0_), channel_id=1, source_target_pairs={{0,1},{1,0},{2,3},{3,2},{4,5},{5,4},{6,7},{7,6},{8,9},{9,8},{10,11... | collective-permute-start | bytes 1572872 | tf_op jit(solution)/shard_map/ppermute | solution.py:39
  119.6 2.0 %collective-permute-start.19 = (bf16[512,512]{1,0:T(8,128)(2,1)S(1)}, bf16[512,512]{1,0:T(8,128)(2,1)}, u32[]{:S(2)}, u32[]{:S(2)}) collective-permute-start(bf16[512,512]{1,0:T(8,128)(2,1)S(1)} %collective-permute-done.18.rest_0_), channel_id=1, source_target_pairs={{0,1},{1,0},{2,3},{3,2},{4,5},{5,4},{6,7},{7,6},{8,9},{9,8},{10,11... | collective-permute-start | bytes 1572872 | tf_op jit(solution)/shard_map/ppermute | solution.py:39
where the time goes:
time: 125 us; the launch traced here: 124 us
  waiting for transfers between devices  73.1 us (58%)
  starting transfers between devices  26 us (21%)
  Pallas kernels  13.3 us (11%)
  local copies, waits for them, and re-layouts  5.75 us (5%)
  matrix products  4.43 us (4%)
    ppermute x12, waiting for transfers between devices, swap(): return lax.ppermute(array, axis, [(i, i ^ mask) for i in range(devices)])  33.7 us
    ppermute x12, starting transfers between devices, swap(): return lax.ppermute(array, axis, [(i, i ^ mask) for i in range(devices)])  17.9 us
    ppermute x1, waiting for transfers between devices, shards(): early_rates = lax.ppermute(rates_row, 'seq', behind)  15.6 us
    ppermute x6, waiting for transfers between devices, ring_step(): return lax.ppermute(unit, 'seq', pairs)  12.7 us
    ppermute x1, waiting for transfers between devices, shards(): early_keys = lax.ppermute(keys, 'seq', behind)  11.1 us
    unnamed x22, local copies, waits for them, and re-layouts  5.02 us
    pallas_call x2, Pallas kernels, project(): pl.pallas_call(functools.partial(project_kernel, count, tags, len(blocks)...  4.59 us
    ppermute x6, starting transfers between devices, ring_step(): return lax.ppermute(unit, 'seq', pairs)  3.99 us
  transfers between devices with their start and end apart: 21, of which 14 were waited for; matrix products, arithmetic and copies ran while one was open for 6% of the time, Pallas kernels for 4%

commit v1 on v0

--- a/solution.py
+++ b/solution.py
@@ -181,9 +181,8 @@
     )(origin, q, attended, *units)
 
 
-def project_kernel(count, tags, blocks_in, last, origin, *rest):
-    blocks, units = rest[:blocks_in], rest[blocks_in : blocks_in + 4]
-    before = None if not last else rest[blocks_in + 4]
+def project_kernel(count, tags, origin, *rest):
+    blocks, units = rest[: len(tags)], rest[len(tags) : len(tags) + 4]
     total, full = rest[-2:]
     steps = count // 2
     rows_in = units[0].shape[0] * 2 // steps
@@ -192,7 +191,7 @@
         rows = pl.ds(pl.multiple_of(origin[i] * rows_in, rows_in), rows_in)
         full[rows, :] = units[2 * (i // steps) + part][pl.ds(at * rows_in, rows_in), :]
     width = blocks[0].shape[1]
-    value = before[...] if last else None
+    value = None
     for block, tag in zip(blocks, tags):
         rows = pl.ds(pl.multiple_of((origin[count] ^ tag) * width, width), width)
         part = matmul(block[...], full[rows, :])
@@ -200,16 +199,15 @@
     total[...] = value.astype(total.dtype)
 
 
-def project(origin, blocks, tags, units, before=None):
+def project(origin, blocks, tags, units):
     tokens = blocks[0].shape[0]
     count = origin.shape[0] - 1
     rows_in, width = sum(unit.shape[0] for unit in units), units[0].shape[1]
-    last = before is not None
     return pl.pallas_call(
-        functools.partial(project_kernel, count, tags, len(blocks), last),
-        out_shape=jax.ShapeDtypeStruct((tokens, width), jnp.bfloat16 if last else jnp.float32),
+        functools.partial(project_kernel, count, tags),
+        out_shape=jax.ShapeDtypeStruct((tokens, width), jnp.bfloat16),
         in_specs=[pl.BlockSpec(memory_space=pltpu.SMEM)]
-        + [whole_spec()] * (4 + len(blocks) + last),
+        + [whole_spec()] * (4 + len(blocks)),
         out_specs=whole_spec(),
         scratch_shapes=[pltpu.VMEM((rows_in, width), jnp.bfloat16)],
         compiler_params=params(14),
@@ -219,7 +217,7 @@
             transcendentals=0,
         ),
         name="project",
-    )(origin, *blocks, *units, *([before] if last else []))
+    )(origin, *blocks, *units)
 
 
 def ring_order(outer):
@@ -288,18 +286,18 @@
 
     behind = [(i, (i + 1) % ranks) for i in range(ranks)]
     rates_row = rates.reshape(1, tok_rows)
+    early_rates = lax.ppermute(rates_row, "seq", behind)
     early_keys = lax.ppermute(keys, "seq", behind)
-    early_values = lax.ppermute(values, "seq", behind)
-    early_rates = lax.ppermute(rates_row, "seq", behind)
+    early_values = lax.ppermute(after(values, early_rates), "seq", behind)
 
     acc = own_gradients(place, keys, values, rates_row, fast, outer, grad_scale)
-    wide = [after(out_proj, acc)]
+    wide = [after(out_proj, early_rates)]
     for _ in range(1, outer):
         wide.append(ring_step(wide[-1], outer))
     half = outer // 2
     near_half = [jnp.concatenate(wide[:half]), jnp.concatenate(wide[half:])]
-    early_keys = after(early_keys, wide[-2])
-    far_half = [swap(unit, "seq", 1) for unit in near_half]
+    early_values = after(early_values, *near_half)
+    far_half = [swap(after(near_half[0], early_keys, early_values), "seq", 1)]
 
     summed = both_gradients(
         place, early_keys, early_values, early_rates, fast, acc, outer, grad_scale
@@ -309,19 +307,19 @@
     total = summed[0]
     for piece in arrived:
         total = total + piece.astype(jnp.float32)
+    attended = attention(queries, keys, values, early_keys, early_values, position)
+    total = after(total, attended)
     moment_own = MOMENTUM_DECAY * momentum[0] + total
     base_rows = lax.dynamic_slice_in_dim(fast[0], position * own_rows, own_rows, 1).astype(jnp.float32)
     near = [renormalize(base_rows, moment_own)]
     far = [swap(near[0], "seq", 1)]
     for step in range(1, outer):
         near.append(ring_step(near[-1], outer))
-        if step == 2:
-            near[-1] = after(near[-1], far_half[1])
         if step > 1:
             near[-1] = after(near[-1], far[step - 2])
         far.append(swap(near[-1], "seq", 1))
-
-    attended = attention(queries, keys, values, early_keys, early_values, position)
+    far_half.append(swap(after(near_half[1], far[-2]), "seq", 1))
+
     combined = apply_fast(origins, queries, attended, near + far)
 
     blocks = [(combined, 0)]
@@ -330,13 +328,9 @@
         blocks = blocks + [(swap(block, "head", mask), tag ^ mask) for block, tag in blocks]
         mask //= 2
     origins = jnp.concatenate([origins, head[None].astype(jnp.int32)])
-    early = [pair for pair in blocks if pair[1] <= 1]
-    late = [pair for pair in blocks if pair[1] > 1]
-    mixed = None
-    for group in (early, late):
-        mixed = project(
-            origins, [b for b, _ in group], [t for _, t in group], near_half + far_half, mixed
-        )
+    mixed = project(
+        origins, [b for b, _ in blocks], [t for _, t in blocks], near_half + far_half
+    )
     return (mixed, moment_own[None])
 
 

time: 125 us -> 122 us (0.976)
  waiting for transfers between devices: 73.1 us -> 57.1 us
  starting transfers between devices: 26 us -> 36 us
  local copies, waits for them, and re-layouts: 5.75 us -> 11.4 us
  Pallas kernels: 13.3 us -> 11.7 us
  matrix products: 4.43 us -> 2.92 us
    ppermute x1, waiting for transfers between devices: 15.6 us -> 3.18 us  [shards(): early_rates = lax.ppermute(rates_row, 'seq', behind)]
    ppermute x12, waiting for transfers between devices: 33.7 us -> 25.1 us  [swap(): return lax.ppermute(array, axis, [(i, i ^ mask) for i in range(devices)])]
    ppermute x1, waiting for transfers between devices: 11.1 us -> 3.2 us  [shards(): early_keys = lax.ppermute(keys, 'seq', behind)]
    ppermute x1, waiting for transfers between devices: 0.01 us -> 7.03 us  [shards(): early_values = lax.ppermute(after(values, early_rates), 'seq', behind)]
    ppermute x6, waiting for transfers between devices: 12.7 us -> 18.6 us  [ring_step(): return lax.ppermute(unit, 'seq', pairs)]
    ppermute x6, starting transfers between devices: 3.99 us -> 9.77 us  [ring_step(): return lax.ppermute(unit, 'seq', pairs)]
    unnamed x22 -> x34, local copies, waits for them, and re-layouts: 5.02 us -> 10.6 us
    ppermute x12, starting transfers between devices: 17.9 us -> 21.1 us  [swap(): return lax.ppermute(array, axis, [(i, i ^ mask) for i in range(devices)])]
  transfers between devices with their start and end apart: 21 -> 21, of which waited for: 14 -> 17; matrix products, arithmetic and copies ran while one was open for 6% -> 3% of each run, Pallas kernels for 4% -> 5%
where the time goes in v1:
time: 122 us
  waiting for transfers between devices  57.1 us (47%)
  starting transfers between devices  36 us (30%)
  Pallas kernels  11.7 us (10%)
  local copies, waits for them, and re-layouts  11.4 us (9%)
  matrix products  2.92 us (2%)
  other arithmetic  1.65 us (1%)
    ppermute x12, waiting for transfers between devices, swap(): return lax.ppermute(array, axis, [(i, i ^ mask) for i in range(devices)])  25.1 us
    ppermute x12, starting transfers between devices, swap(): return lax.ppermute(array, axis, [(i, i ^ mask) for i in range(devices)])  21.1 us
    ppermute x6, waiting for transfers between devices, ring_step(): return lax.ppermute(unit, 'seq', pairs)  18.6 us
    unnamed x34, local copies, waits for them, and re-layouts  10.6 us
    ppermute x6, starting transfers between devices, ring_step(): return lax.ppermute(unit, 'seq', pairs)  9.77 us
    ppermute x1, waiting for transfers between devices, shards(): early_values = lax.ppermute(after(values, early_rates), 'seq', behind)  7.03 us
    pallas_call x1, Pallas kernels, project(): pl.pallas_call(functools.partial(project_kernel, count, tags), out_shape=...  3.39 us
    pallas_call x1, Pallas kernels, own_gradients(): pl.pallas_call(functools.partial(own_kernel, outer, scale), out_shape=jax...  3.31 us
  transfers between devices with their start and end apart: 21, of which 17 were waited for; matrix products, arithmetic and copies ran while one was open for 3% of the time, Pallas kernels for 5%

profile of v1, /device:TPU:0, one launch (start us, length us, event | category | flops | bytes accessed | tf_op | source)
XLA Modules:
  0.0 121.5 jit_solution(17115092835110450075)
XLA Ops:
  0.6 3.0 %collective-permute-start.1 = (f32[1,512]{1,0:T(1,128)}, f32[1,512]{1,0:T(1,128)S(1)}, u32[]{:S(2)}, u32[]{:S(2)}) collective-permute-start(f32[1,512]{1,0:T(1,128)} %bitcast.24), channel_id=1, source_target_pairs={{0,4},{4,8},{8,12},{12,16},{16,20},{20,24},{24,28},{28,0},{1,5},{5... | collective-permute-start | bytes 6152 | tf_op jit(solution)/shard_map/ppermute | solution.py:289
  3.6 1.5 %collective-permute-start = (bf16[512,512]{1,0:T(8,128)(2,1)}, bf16[512,512]{1,0:T(8,128)(2,1)S(1)}, u32[]{:S(2)}, u32[]{:S(2)}) collective-permute-start(bf16[512,512]{1,0:T(8,128)(2,1)} %k.1), channel_id=1, source_target_pairs={{0,4},{4,8},{8,12},{12,16},{16,20},{20,24},{24,28},{28,0},{1,5},{5... | collective-permute-start | bytes 1572872 | tf_op jit(solution)/shard_map/ppermute | solution.py:290
  5.3 3.2 %collective-permute-done.1.r = f32[1,512]{1,0:T(1,128)S(1)} collective-permute-done((f32[1,512]{1,0:T(1,128)}, f32[1,512]{1,0:T(1,128)S(1)}, u32[]{:S(2)}, u32[]{:S(2)}) %collective-permute-start.1) | collective-permute-done | bytes 2080 | tf_op jit(solution)/shard_map/ppermute | solution.py:289
  8.5 1.4 %copy-done.10 = bf16[1,3,512,512]{3,2,1,0:T(8,128)(2,1)S(1)} copy-done((bf16[1,3,512,512]{3,2,1,0:T(8,128)(2,1)S(1)}, bf16[1,3,512,512]{3,2,1,0:T(8,128)(2,1)}, u32[]{:S(2)}) %copy-start.10) | copy-done | bytes 1572888
  9.9 1.0 copy-done.12
  11.6 3.3 %own_gradients.1.acc = f32[4,3,64,512]{3,2,1,0:T(8,128)S(1)} custom-call(s32[2]{0:T(128)S(1)} %pad_add_fusion.1.place, bf16[512,512]{1,0:T(8,128)(2,1)S(1)} %copy-done.12, bf16[512,512]{1,0:T(8,128)(2,1)} %v.1, f32[1,512]{1,0:T(1,128)S(1)} %bitcast.25, bf16[1,3,512,512]{3,2,1,0:T(8,128)(2,1)S(1)} %copy-done.10), custom_call_target="tpu_custom_call" | custom-call | flops 1610612736 | bytes 4000000 | tf_op jit(solution)/shard_map/own_gradients/pallas_call | solution.py:127
  15.5 1.2 collective-permute-done.3
  16.8 1.5 %collective-permute-start.4 = (bf16[256,512]{1,0:T(8,128)(2,1)S(1)}, bf16[256,512]{1,0:T(8,128)(2,1)S(1)}, u32[]{:S(2)}, u32[]{:S(2)}) collective-permute-start(bf16[256,512]{1,0:T(8,128)(2,1)S(1)} %collective-permute-done.3), channel_id=1, source_target_pairs={{0,8},{4,12},{8,24},{12,28},{24,16},{28,20},{16,0},{20,4},{1,9},{5... | collective-permute-start | bytes 786440 | tf_op jit(solution)/shard_map/ppermute | solution.py:233
  18.2 3.2 %collective-permute-done.k = bf16[512,512]{1,0:T(8,128)(2,1)S(1)} collective-permute-done((bf16[512,512]{1,0:T(8,128)(2,1)}, bf16[512,512]{1,0:T(8,128)(2,1)S(1)}, u32[]{:S(2)}, u32[]{:S(2)}) %collective-permute-start) | collective-permute-done | bytes 524320 | tf_op jit(solution)/shard_map/ppermute | solution.py:290
  21.5 1.1 fusion.15
  22.6 1.4 %collective-permute-done.4 = bf16[256,512]{1,0:T(8,128)(2,1)S(1)} collective-permute-done((bf16[256,512]{1,0:T(8,128)(2,1)S(1)}, bf16[256,512]{1,0:T(8,128)(2,1)S(1)}, u32[]{:S(2)}, u32[]{:S(2)}) %collective-permute-start.4) | collective-permute-done | bytes 262176 | tf_op jit(solution)/shard_map/ppermute | solution.py:233
  25.4 5.9 %collective-permute-done.5 = bf16[256,512]{1,0:T(8,128)(2,1)S(1)} collective-permute-done((bf16[256,512]{1,0:T(8,128)(2,1)S(1)}, bf16[256,512]{1,0:T(8,128)(2,1)S(1)}, u32[]{:S(2)}, u32[]{:S(2)}) %collective-permute-start.5) | collective-permute-done | bytes 262176 | tf_op jit(solution)/shard_map/ppermute | solution.py:233
  31.3 7.0 %collective-permute-done.2.v = bf16[512,512]{1,0:T(8,128)(2,1)S(1)} collective-permute-done((bf16[512,512]{1,0:T(8,128)(2,1)}, bf16[512,512]{1,0:T(8,128)(2,1)S(1)}, u32[]{:S(2)}, u32[]{:S(2)}) %collective-permute-start.2) | collective-permute-done | bytes 524320 | tf_op jit(solution)/shard_map/ppermute | solution.py:291
  38.3 13.9 %collective-permute-start.7 = (bf16[512,512]{1,0:T(8,128)(2,1)S(1)}, bf16[512,512]{1,0:T(8,128)(2,1)S(1)}, u32[]{:S(2)}, u32[]{:S(2)}) collective-permute-start(bf16[512,512]{1,0:T(8,128)(2,1)S(1)} %constant_dynamic-update-slice_fusion.rest_4_), channel_id=1, source_target_pairs={{0,4},{4,0},{8,12},{12,8},{16,20},{20,16},{24,28},{28,24},{1,5},{5... | collective-permute-start | bytes 1572872 | tf_op jit(solution)/shard_map/ppermute | solution.py:39
  52.2 2.8 %both_gradients.1 = (f32[3,64,512]{2,1,0:T(8,128)S(1)}, bf16[3,64,512]{2,1,0:T(8,128)(2,1)S(1)}, bf16[3,64,512]{2,1,0:T(8,128)(2,1)S(1)}, bf16[3,64,512]{2,1,0:T(8,128)(2,1)S(1)}) custom-call(s32[2]{0:T(128)S(1)} %pad_add_fusion.1.place, bf16[512,512]{1,0:T(8,128)(2,1)S(1)} %collective-permute-done.k, bf16[512,512]{1,0:T(8,128)(2,1)S(1)} %collective-permute-done.2.v, ...), custom_call_target="tpu_custom_call" | custom-call | flops 1610612736 | bytes 4000000 | tf_op jit(solution)/shard_map/both_gradients/pallas_call | solution.py:142
  56.1 3.5 %collective-permute-start.9 = (bf16[3,64,512]{2,1,0:T(8,128)(2,1)S(1)}, bf16[3,64,512]{2,1,0:T(8,128)(2,1)S(1)}, u32[]{:S(2)}, u32[]{:S(2)}) collective-permute-start(bf16[3,64,512]{2,1,0:T(8,128)(2,1)S(1)} %get-tuple-element.23), channel_id=1, source_target_pairs={{0,24},{4,28},{8,16},{12,20},{16,8},{20,12},{24,0},{28,4},{1,25},{... | collective-permute-start | bytes 589832 | tf_op jit(solution)/shard_map/ppermute | solution.py:39
  59.5 1.8 %fusion.6.attended = f32[512,512]{1,0:T(8,128)S(1)} fusion(bf16[512,512]{1,0:T(8,128)(2,1)} %v.1, bf16[512,512]{1,0:T(8,128)(2,1)S(1)} %collective-permute-done.2.v, f32[512,1024]{0,1:T(8,128)S(1)} %get-tuple-element.33, f32[512]{0:T(512)S(1)} %fusion.2, f32[512]{0:T(512)S(1)} %get-tuple-element.32), kind=kOutput, calls=%fused_computation.11 | convolution fusion | flops 540540928 | bytes 4198400 | tf_op jit(solution)/shard_map/dot_general | solution.py:270
  61.3 2.1 %collective-permute-done.6 = bf16[3,64,512]{2,1,0:T(8,128)(2,1)S(1)} collective-permute-done((bf16[3,64,512]{2,1,0:T(8,128)(2,1)S(1)}, bf16[3,64,512]{2,1,0:T(8,128)(2,1)S(1)}, u32[]{:S(2)}, u32[]{:S(2)}) %collective-permute-start.6) | collective-permute-done | bytes 196640 | tf_op jit(solution)/shard_map/ppermute | solution.py:39
  63.5 8.4 %collective-permute-done.8 = bf16[3,64,512]{2,1,0:T(8,128)(2,1)S(1)} collective-permute-done((bf16[3,64,512]{2,1,0:T(8,128)(2,1)S(1)}, bf16[3,64,512]{2,1,0:T(8,128)(2,1)S(1)}, u32[]{:S(2)}, u32[]{:S(2)}) %collective-permute-start.8) | collective-permute-done | bytes 196640 | tf_op jit(solution)/shard_map/ppermute | solution.py:39
  73.1 3.2 %collective-permute-start.10 = (bf16[3,64,512]{2,1,0:T(8,128)(2,1)S(1)}, bf16[3,64,512]{2,1,0:T(8,128)(2,1)S(1)}, u32[]{:S(2)}, u32[]{:S(2)}) collective-permute-start(bf16[3,64,512]{2,1,0:T(8,128)(2,1)S(1)} %get-tuple-element.31.rest_0_), channel_id=1, source_target_pairs={{0,8},{4,12},{8,24},{12,28},{24,16},{28,20},{16,0},{20,4},{1,9},{5... | collective-permute-start | bytes 589832 | tf_op jit(solution)/shard_map/ppermute | solution.py:233
  76.5 3.3 %collective-permute-done.10.rest_1_ = bf16[3,64,512]{2,1,0:T(8,128)(2,1)S(1)} collective-permute-done((bf16[3,64,512]{2,1,0:T(8,128)(2,1)S(1)}, bf16[3,64,512]{2,1,0:T(8,128)(2,1)S(1)}, u32[]{:S(2)}, u32[]{:S(2)}) %collective-permute-start.10) | collective-permute-done | bytes 196640 | tf_op jit(solution)/shard_map/ppermute | solution.py:233
  79.8 2.1 %collective-permute-start.11 = (bf16[3,64,512]{2,1,0:T(8,128)(2,1)S(1)}, bf16[3,64,512]{2,1,0:T(8,128)(2,1)S(1)}, u32[]{:S(2)}, u32[]{:S(2)}) collective-permute-start(bf16[3,64,512]{2,1,0:T(8,128)(2,1)S(1)} %collective-permute-done.10.rest_1_), channel_id=1, source_target_pairs={{0,8},{4,12},{8,24},{12,28},{24,16},{28,20},{16,0},{20,4},{1,9},{5... | collective-permute-start | bytes 589832 | tf_op jit(solution)/shard_map/ppermute | solution.py:233
  82.9 3.8 %collective-permute-done.11.rest_2_ = bf16[3,64,512]{2,1,0:T(8,128)(2,1)S(1)} collective-permute-done((bf16[3,64,512]{2,1,0:T(8,128)(2,1)S(1)}, bf16[3,64,512]{2,1,0:T(8,128)(2,1)S(1)}, u32[]{:S(2)}, u32[]{:S(2)}) %collective-permute-start.11) | collective-permute-done | bytes 196640 | tf_op jit(solution)/shard_map/ppermute | solution.py:233
  86.7 2.0 %collective-permute-start.13 = (bf16[3,64,512]{2,1,0:T(8,128)(2,1)S(1)}, bf16[3,64,512]{2,1,0:T(8,128)(2,1)}, u32[]{:S(2)}, u32[]{:S(2)}) collective-permute-start(bf16[3,64,512]{2,1,0:T(8,128)(2,1)S(1)} %collective-permute-done.11.rest_2_), channel_id=1, source_target_pairs={{0,8},{4,12},{8,24},{12,28},{24,16},{28,20},{16,0},{20,4},{1,9},{5... | collective-permute-start | bytes 589832 | tf_op jit(solution)/shard_map/ppermute | solution.py:233
  90.3 3.0 %collective-permute-done.13.rest_3_ = bf16[3,64,512]{2,1,0:T(8,128)(2,1)} collective-permute-done((bf16[3,64,512]{2,1,0:T(8,128)(2,1)S(1)}, bf16[3,64,512]{2,1,0:T(8,128)(2,1)}, u32[]{:S(2)}, u32[]{:S(2)}) %collective-permute-start.13) | collective-permute-done | bytes 196640 | tf_op jit(solution)/shard_map/ppermute | solution.py:233
  94.2 1.3 %collective-permute-done.15.rest_6_ = bf16[3,64,512]{2,1,0:T(8,128)(2,1)} collective-permute-done((bf16[3,64,512]{2,1,0:T(8,128)(2,1)S(1)}, bf16[3,64,512]{2,1,0:T(8,128)(2,1)}, u32[]{:S(2)}, u32[]{:S(2)}) %collective-permute-start.15) | collective-permute-done | bytes 196640 | tf_op jit(solution)/shard_map/ppermute | solution.py:39
  95.5 3.7 %collective-permute-done.16.rest_7_ = bf16[3,64,512]{2,1,0:T(8,128)(2,1)S(1)} collective-permute-done((bf16[3,64,512]{2,1,0:T(8,128)(2,1)}, bf16[3,64,512]{2,1,0:T(8,128)(2,1)S(1)}, u32[]{:S(2)}, u32[]{:S(2)}) %collective-permute-start.16) | collective-permute-done | bytes 196640 | tf_op jit(solution)/shard_map/ppermute | solution.py:39
  104.7 2.2 %apply_fast.1.rest_0_ = bf16[512,512]{1,0:T(8,128)(2,1)S(1)} custom-call(s32[8]{0:T(128)S(1)} %dynamic-slice_bitcast_fusion.origin, bf16[512,512]{1,0:T(8,128)(2,1)S(1)} %copy-done.1, f32[512,512]{1,0:T(8,128)S(1)} %fusion.6.attended, bf16[3,64,512]{2,1,0:T(8,128)(2,1)S(1)} %get-tuple-element.31.rest_0_, ...), custom_call_target="tpu_custom_call" | custom-call | flops 805306368 | bytes 4000000 | tf_op jit(solution)/shard_map/apply_fast/pallas_call | solution.py:170
  106.8 1.6 %collective-permute-start.17 = (bf16[512,512]{1,0:T(8,128)(2,1)S(1)}, bf16[512,512]{1,0:T(8,128)(2,1)S(1)}, u32[]{:S(2)}, u32[]{:S(2)}) collective-permute-start(bf16[512,512]{1,0:T(8,128)(2,1)S(1)} %apply_fast.1.rest_0_), channel_id=1, source_target_pairs={{0,2},{1,3},{2,0},{3,1},{4,6},{5,7},{6,4},{7,5},{8,10},{9,11},{10,... | collective-permute-start | bytes 1572872 | tf_op jit(solution)/shard_map/ppermute | solution.py:39
  108.5 7.5 %collective-permute-done.17.rest_1_ = bf16[512,512]{1,0:T(8,128)(2,1)S(1)} collective-permute-done((bf16[512,512]{1,0:T(8,128)(2,1)S(1)}, bf16[512,512]{1,0:T(8,128)(2,1)S(1)}, u32[]{:S(2)}, u32[]{:S(2)}) %collective-permute-start.17) | collective-permute-done | bytes 524320 | tf_op jit(solution)/shard_map/ppermute | solution.py:39
  116.1 1.4 %collective-permute-done.20.rest_7_ = bf16[512,512]{1,0:T(8,128)(2,1)S(1)} collective-permute-done((bf16[512,512]{1,0:T(8,128)(2,1)S(1)}, bf16[512,512]{1,0:T(8,128)(2,1)S(1)}, u32[]{:S(2)}, u32[]{:S(2)}) %collective-permute-start.20) | collective-permute-done | bytes 524320 | tf_op jit(solution)/shard_map/ppermute | solution.py:39
  118.1 3.4 %project.1 = bf16[512,512]{1,0:T(8,128)(2,1)} custom-call(s32[9]{0:T(128)S(1)} %pad_add_fusion.origin, bf16[512,512]{1,0:T(8,128)(2,1)S(1)} %apply_fast.1.rest_0_, bf16[512,512]{1,0:T(8,128)(2,1)S(1)} %collective-permute-done.17.rest_1_, bf16[512,512]{1,0:T(8,128)(2,1)} %collective-permute-done.18.rest_2_, bf16[512,512]{1,0:T(8,128)(2,1)} %collective-permute-done.19.rest_3_, ...), custom_call_target="tpu_custom_call" | custom-call | flops 1073741824 | bytes 4000000 | tf_op jit(solution)/shard_map/project/pallas_call | solution.py:206
  (63 shorter events, 14.9 us)
Async XLA Ops:
  0.6 7.8 %collective-permute-start.1 = (f32[1,512]{1,0:T(1,128)}, f32[1,512]{1,0:T(1,128)S(1)}, u32[]{:S(2)}, u32[]{:S(2)}) collective-permute-start(f32[1,512]{1,0:T(1,128)} %bitcast.24), channel_id=1, source_target_pairs={{0,4},{4,8},{8,12},{12,16},{16,20},{20,24},{24,28},{28,0},{1,5},{5... | collective-permute-start | bytes 6152 | tf_op jit(solution)/shard_map/ppermute | solution.py:289
  3.6 17.8 %collective-permute-start = (bf16[512,512]{1,0:T(8,128)(2,1)}, bf16[512,512]{1,0:T(8,128)(2,1)S(1)}, u32[]{:S(2)}, u32[]{:S(2)}) collective-permute-start(bf16[512,512]{1,0:T(8,128)(2,1)} %k.1), channel_id=1, source_target_pairs={{0,4},{4,8},{8,12},{12,16},{16,20},{20,24},{24,28},{28,0},{1,5},{5... | collective-permute-start | bytes 1572872 | tf_op jit(solution)/shard_map/ppermute | solution.py:290
  5.3 16.2 %copy-start = (bf16[512,512]{1,0:T(8,128)(2,1)S(1)}, bf16[512,512]{1,0:T(8,128)(2,1)}, u32[]{:S(2)}) copy-start(bf16[512,512]{1,0:T(8,128)(2,1)} %q.1) | copy-start | bytes 1572868
  8.5 8.3 %collective-permute-start.3 = (bf16[256,512]{1,0:T(8,128)(2,1)}, bf16[256,512]{1,0:T(8,128)(2,1)S(1)}, u32[]{:S(2)}, u32[]{:S(2)}) collective-permute-start(bf16[256,512]{1,0:T(8,128)(2,1)} %param.14), channel_id=1, source_target_pairs={{0,8},{4,12},{8,24},{12,28},{24,16},{28,20},{16,0},{20,4},{1,9},{5... | collective-permute-start | bytes 786440 | tf_op jit(solution)/shard_map/ppermute | solution.py:233
  8.5 1.4 %copy-start.10 = (bf16[1,3,512,512]{3,2,1,0:T(8,128)(2,1)S(1)}, bf16[1,3,512,512]{3,2,1,0:T(8,128)(2,1)}, u32[]{:S(2)}) copy-start(bf16[1,3,512,512]{3,2,1,0:T(8,128)(2,1)} %w.3) | copy-start | bytes 4718596
  9.9 1.0 copy-start.12
  11.6 3.9 %copy-start.15 = (bf16[256,512]{1,0:T(8,128)(2,1)S(1)}, bf16[256,512]{1,0:T(8,128)(2,1)}, u32[]{:S(2)}) copy-start(bf16[256,512]{1,0:T(8,128)(2,1)} %param.14) | copy-start | bytes 786436
  14.9 23.4 %collective-permute-start.2 = (bf16[512,512]{1,0:T(8,128)(2,1)}, bf16[512,512]{1,0:T(8,128)(2,1)S(1)}, u32[]{:S(2)}, u32[]{:S(2)}) collective-permute-start(bf16[512,512]{1,0:T(8,128)(2,1)} %v.1), channel_id=1, source_target_pairs={{0,4},{4,8},{8,12},{12,16},{16,20},{20,24},{24,28},{28,0},{1,5},{5... | collective-permute-start | bytes 1572872 | tf_op jit(solution)/shard_map/ppermute | solution.py:291
  16.8 7.3 %collective-permute-start.4 = (bf16[256,512]{1,0:T(8,128)(2,1)S(1)}, bf16[256,512]{1,0:T(8,128)(2,1)S(1)}, u32[]{:S(2)}, u32[]{:S(2)}) collective-permute-start(bf16[256,512]{1,0:T(8,128)(2,1)S(1)} %collective-permute-done.3), channel_id=1, source_target_pairs={{0,8},{4,12},{8,24},{12,28},{24,16},{28,20},{16,0},{20,4},{1,9},{5... | collective-permute-start | bytes 786440 | tf_op jit(solution)/shard_map/ppermute | solution.py:233
  22.6 29.7 %copy-start.11 = (bf16[1,3,512,512]{3,2,1,0:T(8,128)(2,1)S(1)}, bf16[1,3,512,512]{3,2,1,0:T(8,128)(2,1)}, u32[]{:S(2)}) copy-start(bf16[1,3,512,512]{3,2,1,0:T(8,128)(2,1)} %w.3) | copy-start | bytes 4718596
  24.0 7.3 %collective-permute-start.5 = (bf16[256,512]{1,0:T(8,128)(2,1)S(1)}, bf16[256,512]{1,0:T(8,128)(2,1)S(1)}, u32[]{:S(2)}, u32[]{:S(2)}) collective-permute-start(bf16[256,512]{1,0:T(8,128)(2,1)S(1)} %collective-permute-done.4), channel_id=1, source_target_pairs={{0,8},{4,12},{8,24},{12,28},{24,16},{28,20},{16,0},{20,4},{1,9},{5... | collective-permute-start | bytes 786440 | tf_op jit(solution)/shard_map/ppermute | solution.py:233
  38.3 25.2 %collective-permute-start.7 = (bf16[512,512]{1,0:T(8,128)(2,1)S(1)}, bf16[512,512]{1,0:T(8,128)(2,1)S(1)}, u32[]{:S(2)}, u32[]{:S(2)}) collective-permute-start(bf16[512,512]{1,0:T(8,128)(2,1)S(1)} %constant_dynamic-update-slice_fusion.rest_4_), channel_id=1, source_target_pairs={{0,4},{4,0},{8,12},{12,8},{16,20},{20,16},{24,28},{28,24},{1,5},{5... | collective-permute-start | bytes 1572872 | tf_op jit(solution)/shard_map/ppermute | solution.py:39
  55.1 8.3 %collective-permute-start.6 = (bf16[3,64,512]{2,1,0:T(8,128)(2,1)S(1)}, bf16[3,64,512]{2,1,0:T(8,128)(2,1)S(1)}, u32[]{:S(2)}, u32[]{:S(2)}) collective-permute-start(bf16[3,64,512]{2,1,0:T(8,128)(2,1)S(1)} %get-tuple-element.19), channel_id=1, source_target_pairs={{0,8},{4,12},{8,0},{12,4},{16,24},{20,28},{24,16},{28,20},{1,9},{5... | collective-permute-start | bytes 589832 | tf_op jit(solution)/shard_map/ppermute | solution.py:39
  55.2 16.7 %collective-permute-start.8 = (bf16[3,64,512]{2,1,0:T(8,128)(2,1)S(1)}, bf16[3,64,512]{2,1,0:T(8,128)(2,1)S(1)}, u32[]{:S(2)}, u32[]{:S(2)}) collective-permute-start(bf16[3,64,512]{2,1,0:T(8,128)(2,1)S(1)} %get-tuple-element.22), channel_id=1, source_target_pairs={{0,16},{4,20},{8,24},{12,28},{16,0},{20,4},{24,8},{28,12},{1,17},{... | collective-permute-start | bytes 589832 | tf_op jit(solution)/shard_map/ppermute | solution.py:39
  56.1 16.0 %copy-start.14 = (f32[1,3,64,512]{3,2,1,0:T(8,128)S(1)}, f32[1,3,64,512]{3,2,1,0:T(8,128)}, u32[]{:S(2)}) copy-start(f32[1,3,64,512]{3,2,1,0:T(8,128)} %param.13) | copy-start | bytes 1179652
  56.1 15.9 %collective-permute-start.9 = (bf16[3,64,512]{2,1,0:T(8,128)(2,1)S(1)}, bf16[3,64,512]{2,1,0:T(8,128)(2,1)S(1)}, u32[]{:S(2)}, u32[]{:S(2)}) collective-permute-start(bf16[3,64,512]{2,1,0:T(8,128)(2,1)S(1)} %get-tuple-element.23), channel_id=1, source_target_pairs={{0,24},{4,28},{8,16},{12,20},{16,8},{20,12},{24,0},{28,4},{1,25},{... | collective-permute-start | bytes 589832 | tf_op jit(solution)/shard_map/ppermute | solution.py:39
  73.1 6.7 %collective-permute-start.10 = (bf16[3,64,512]{2,1,0:T(8,128)(2,1)S(1)}, bf16[3,64,512]{2,1,0:T(8,128)(2,1)S(1)}, u32[]{:S(2)}, u32[]{:S(2)}) collective-permute-start(bf16[3,64,512]{2,1,0:T(8,128)(2,1)S(1)} %get-tuple-element.31.rest_0_), channel_id=1, source_target_pairs={{0,8},{4,12},{8,24},{12,28},{24,16},{28,20},{16,0},{20,4},{1,9},{5... | collective-permute-start | bytes 589832 | tf_op jit(solution)/shard_map/ppermute | solution.py:233
  76.2 6.0 %collective-permute-start.12 = (bf16[3,64,512]{2,1,0:T(8,128)(2,1)S(1)}, bf16[3,64,512]{2,1,0:T(8,128)(2,1)S(1)}, u32[]{:S(2)}, u32[]{:S(2)}) collective-permute-start(bf16[3,64,512]{2,1,0:T(8,128)(2,1)S(1)} %get-tuple-element.31.rest_0_), channel_id=1, source_target_pairs={{0,4},{4,0},{8,12},{12,8},{16,20},{20,16},{24,28},{28,24},{1,5},{5... | collective-permute-start | bytes 589832 | tf_op jit(solution)/shard_map/ppermute | solution.py:39
  79.8 6.9 %collective-permute-start.11 = (bf16[3,64,512]{2,1,0:T(8,128)(2,1)S(1)}, bf16[3,64,512]{2,1,0:T(8,128)(2,1)S(1)}, u32[]{:S(2)}, u32[]{:S(2)}) collective-permute-start(bf16[3,64,512]{2,1,0:T(8,128)(2,1)S(1)} %collective-permute-done.10.rest_1_), channel_id=1, source_target_pairs={{0,8},{4,12},{8,24},{12,28},{24,16},{28,20},{16,0},{20,4},{1,9},{5... | collective-permute-start | bytes 589832 | tf_op jit(solution)/shard_map/ppermute | solution.py:233
  81.9 7.7 %collective-permute-start.14 = (bf16[3,64,512]{2,1,0:T(8,128)(2,1)S(1)}, bf16[3,64,512]{2,1,0:T(8,128)(2,1)S(1)}, u32[]{:S(2)}, u32[]{:S(2)}) collective-permute-start(bf16[3,64,512]{2,1,0:T(8,128)(2,1)S(1)} %collective-permute-done.10.rest_1_), channel_id=1, source_target_pairs={{0,4},{4,0},{8,12},{12,8},{16,20},{20,16},{24,28},{28,24},{1,5},{5... | collective-permute-start | bytes 589832 | tf_op jit(solution)/shard_map/ppermute | solution.py:39
  86.7 6.7 %collective-permute-start.13 = (bf16[3,64,512]{2,1,0:T(8,128)(2,1)S(1)}, bf16[3,64,512]{2,1,0:T(8,128)(2,1)}, u32[]{:S(2)}, u32[]{:S(2)}) collective-permute-start(bf16[3,64,512]{2,1,0:T(8,128)(2,1)S(1)} %collective-permute-done.11.rest_2_), channel_id=1, source_target_pairs={{0,8},{4,12},{8,24},{12,28},{24,16},{28,20},{16,0},{20,4},{1,9},{5... | collective-permute-start | bytes 589832 | tf_op jit(solution)/shard_map/ppermute | solution.py:233
  88.7 6.8 %collective-permute-start.15 = (bf16[3,64,512]{2,1,0:T(8,128)(2,1)S(1)}, bf16[3,64,512]{2,1,0:T(8,128)(2,1)}, u32[]{:S(2)}, u32[]{:S(2)}) collective-permute-start(bf16[3,64,512]{2,1,0:T(8,128)(2,1)S(1)} %collective-permute-done.11.rest_2_), channel_id=1, source_target_pairs={{0,4},{4,0},{8,12},{12,8},{16,20},{20,16},{24,28},{28,24},{1,5},{5... | collective-permute-start | bytes 589832 | tf_op jit(solution)/shard_map/ppermute | solution.py:39
  93.3 5.9 %collective-permute-start.16 = (bf16[3,64,512]{2,1,0:T(8,128)(2,1)}, bf16[3,64,512]{2,1,0:T(8,128)(2,1)S(1)}, u32[]{:S(2)}, u32[]{:S(2)}) collective-permute-start(bf16[3,64,512]{2,1,0:T(8,128)(2,1)} %collective-permute-done.13.rest_3_), channel_id=1, source_target_pairs={{0,4},{4,0},{8,12},{12,8},{16,20},{20,16},{24,28},{28,24},{1,5},{5... | collective-permute-start | bytes 589832 | tf_op jit(solution)/shard_map/ppermute | solution.py:39
  99.9 1.0 copy-start.1
  101.0 0.9 copy-start.3
  101.9 0.9 copy-start.5
  102.8 0.9 copy-start.7
  103.7 0.9 copy-start.9
  106.8 9.2 %collective-permute-start.17 = (bf16[512,512]{1,0:T(8,128)(2,1)S(1)}, bf16[512,512]{1,0:T(8,128)(2,1)S(1)}, u32[]{:S(2)}, u32[]{:S(2)}) collective-permute-start(bf16[512,512]{1,0:T(8,128)(2,1)S(1)} %apply_fast.1.rest_0_), channel_id=1, source_target_pairs={{0,2},{1,3},{2,0},{3,1},{4,6},{5,7},{6,4},{7,5},{8,10},{9,11},{10,... | collective-permute-start | bytes 1572872 | tf_op jit(solution)/shard_map/ppermute | solution.py:39
  108.4 9.2 %collective-permute-start.20 = (bf16[512,512]{1,0:T(8,128)(2,1)S(1)}, bf16[512,512]{1,0:T(8,128)(2,1)S(1)}, u32[]{:S(2)}, u32[]{:S(2)}) collective-permute-start(bf16[512,512]{1,0:T(8,128)(2,1)S(1)} %constant_dynamic-update-slice_fusion.2.rest_5_), channel_id=1, source_target_pairs={{0,4},{4,0},{8,12},{12,8},{16,20},{20,16},{24,28},{28,24},{1,5},{5... | collective-permute-start | bytes 1572872 | tf_op jit(solution)/shard_map/ppermute | solution.py:39
  108.5 9.0 %collective-permute-start.18 = (bf16[512,512]{1,0:T(8,128)(2,1)S(1)}, bf16[512,512]{1,0:T(8,128)(2,1)}, u32[]{:S(2)}, u32[]{:S(2)}) collective-permute-start(bf16[512,512]{1,0:T(8,128)(2,1)S(1)} %apply_fast.1.rest_0_), channel_id=1, source_target_pairs={{0,1},{1,0},{2,3},{3,2},{4,5},{5,4},{6,7},{7,6},{8,9},{9,8},{10,11... | collective-permute-start | bytes 1572872 | tf_op jit(solution)/shard_map/ppermute | solution.py:39
  116.1 2.0 %collective-permute-start.19 = (bf16[512,512]{1,0:T(8,128)(2,1)S(1)}, bf16[512,512]{1,0:T(8,128)(2,1)}, u32[]{:S(2)}, u32[]{:S(2)}) collective-permute-start(bf16[512,512]{1,0:T(8,128)(2,1)S(1)} %collective-permute-done.17.rest_1_), channel_id=1, source_target_pairs={{0,1},{1,0},{2,3},{3,2},{4,5},{5,4},{6,7},{7,6},{8,9},{9,8},{10,11... | collective-permute-start | bytes 1572872 | tf_op jit(solution)/shard_map/ppermute | solution.py:39
  (5 other events, 3.4 us)
